TPU v7x, 128 devices: a whole 4x4x4 slice. The times are simulated.
128 devices in a mesh: dp: 32 (over z, x, y_lo), pool: 4 (over y_hi, core).
Axes of the slice: x: 4, y: 4 (y_hi: 2, y_lo: 2; y = y_hi * 2 + y_lo), z: 4, core: 2. Of those that a mesh axis runs over, the one named last changes fastest.
Arguments:
- pool_image: bfloat16 [98304, 1152], P(('dp', 'pool')), may hold values from -0.23925781 to 0.23925781
- pool_text: bfloat16 [98304, 1152], P(('dp', 'pool')), may hold values from -0.23925781 to 0.23925781
- owners: int32 [32768, 1], P(('dp', 'pool')), may hold values from 0 to 127; in each aligned block of 256 rows (0 to 255, 256 to 511, ...) at most 4 rows name the same one
- slot_index: int32 [32768], P(('dp', 'pool')), may hold values from 0 to 767
Outputs:
- grad_image: float32 [32768, 1152], P(('dp', 'pool'))
- grad_text: float32 [32768, 1152], P(('dp', 'pool'))
Inputs may be any that keep to these rules, and one draw needn't show every extreme that they name: `owners`: among the 256 rows of one device at most 4 name the same owner.
All inputs are finite; a program needn't handle non-finite values.
Results may differ from a plain program's by a relative error of at most 0.0042.
Values may be sent and summed in bfloat16 or wider, within the bound.
A program may use at most 64 MiB of HBM per device.

v0:
```python
import jax
import jax.numpy as jnp
from jax import lax
from jax.sharding import PartitionSpec as P

CYCLE_STEPS = 2


logit_scale = 10.0
logit_bias = -2.0
norm_eps = 1e-06


def passed_along(block, axis, distance):
    devices = range(lax.axis_size(axis))
    route = [((i - distance) % len(devices), i) for i in devices]
    return lax.ppermute(block, axis, route)


def normalize(values):
    widened = values.astype(jnp.float32)
    inverse = lax.rsqrt(jnp.sum(widened * widened, axis=-1, keepdims=True) + norm_eps)
    return (widened * inverse, inverse)


def unnormalize(unit_rows, inverse, upstream):
    return inverse * (upstream - unit_rows * jnp.sum(unit_rows * upstream, axis=-1, keepdims=True))


def sigmoid_weights(image_unit, text_unit, positive):
    logits = (
        logit_scale
        * lax.dot_general(
            image_unit, text_unit, (((1,), (1,)), ((), ())), preferred_element_type=jnp.float32
        )
        + logit_bias
    )
    row_count = logits.shape[0]
    labels = (
        lax.broadcasted_iota(jnp.int32, (row_count, row_count), 0)
        == lax.broadcasted_iota(jnp.int32, (row_count, row_count), 1)
    ).astype(jnp.float32)
    return (jax.nn.sigmoid(logits) - positive * labels).astype(jnp.bfloat16)


def image_side(weights, text_unit):
    return logit_scale * jnp.dot(weights, text_unit, preferred_element_type=jnp.float32)


def text_side(weights, image_unit):
    return logit_scale * lax.dot_general(
        weights, image_unit, (((0,), (0,)), ((), ())), preferred_element_type=jnp.float32
    )


def shards(pool_image, pool_text, owners, slot_index):
    rows_here = slot_index.shape[0]
    devices_all = lax.axis_size(("dp", "pool"))
    capacity = 2 * rows_here // devices_all
    target = owners[:, 0]
    columns = lax.broadcasted_iota(jnp.int32, (rows_here, devices_all), 1)
    one_hot = (target[:, None] == columns).astype(jnp.float32)
    earlier = (
        lax.broadcasted_iota(jnp.int32, (rows_here, rows_here), 0)
        > lax.broadcasted_iota(jnp.int32, (rows_here, rows_here), 1)
    ).astype(jnp.float32)
    before = jnp.dot(
        earlier, one_hot, precision=lax.Precision.HIGHEST, preferred_element_type=jnp.float32
    )
    position = jnp.sum(before * one_hot, axis=1).astype(jnp.int32)
    slot_place = target * capacity + position
    requests = (
        jnp.zeros((devices_all * capacity,), jnp.int32)
        .at[slot_place]
        .set(slot_index)
        .reshape(devices_all, capacity)
    )
    asked_slots = lax.all_to_all(
        requests, ("dp", "pool"), split_axis=0, concat_axis=0, tiled=True
    ).reshape(-1)
    image_rows = pool_image[asked_slots].reshape(devices_all, capacity, -1)
    text_rows = pool_text[asked_slots].reshape(devices_all, capacity, -1)
    image_back, text_back = (
        lax.all_to_all(image_rows, ("dp", "pool"), split_axis=0, concat_axis=0, tiled=True),
        lax.all_to_all(text_rows, ("dp", "pool"), split_axis=0, concat_axis=0, tiled=True),
    )
    image_fetched = image_back.reshape(devices_all * capacity, -1)[slot_place]
    text_fetched = text_back.reshape(devices_all * capacity, -1)[slot_place]
    image_float, image_inverse = normalize(image_fetched)
    text_float, text_inverse = normalize(text_fetched)
    image_unit = image_float.astype(jnp.bfloat16)
    text_unit = text_float.astype(jnp.bfloat16)
    partners = [text_unit]
    for offset in range(CYCLE_STEPS):
        partners.append(passed_along(partners[-1], "dp", 1))
    image_total = jnp.zeros(image_float.shape, jnp.float32)
    text_parts = []
    for offset in range(CYCLE_STEPS + 1):
        weights = sigmoid_weights(image_unit, partners[offset], 1.0 if offset == 0 else 0.0)
        image_total = image_total + image_side(weights, partners[offset])
        text_parts.append(text_side(weights, image_unit))
    text_total = text_parts[0]
    for offset in range(1, CYCLE_STEPS + 1):
        text_total = text_total + passed_along(text_parts[offset], "dp", -offset)
    grad_image = unnormalize(image_float, image_inverse, image_total)
    grad_text = unnormalize(text_float, text_inverse, text_total)
    return (grad_image, grad_text)


def solution(mesh):
    in_specs = (
        P(("dp", "pool"), None),
        P(("dp", "pool"), None),
        P(("dp", "pool"), None),
        P(("dp", "pool")),
    )
    out_specs = (P(("dp", "pool"), None), P(("dp", "pool"), None))
    return jax.shard_map(shards, mesh=mesh, in_specs=in_specs, out_specs=out_specs, check_vma=False)
```

profile of v0, /device:TPU:0, one launch (start us, length us, event | category | flops | bytes accessed | tf_op | source)
XLA Modules:
  0.0 160.3 jit_solution(13931885981147488891)
XLA Ops:
  0.6 0.0 copy-start
  0.6 1.1 fusion.36
  1.7 0.7 compare_select_fusion.1
  2.4 1.6 scatter_custom_fusion
  4.0 0.1 all_to_all.12
  4.1 20.3 %all_to_all.19 = s32[128,1,4]{2,1,0:T(1,128)S(1)} all-to-all(s32[128,1,4]{2,1,0:T(1,128)S(1)} %bitcast.18), channel_id=1, replica_groups=mesh['dp'=32,'pool'=4] {'dp','pool'}, dimensions={0} | all-to-all | bytes 4096 | tf_op jit(solution)/shard_map/all_to_all | solution.py:78
  24.3 0.5 broadcast.111
  24.8 0.8 reduce.3
  25.7 0.1 reshape.74
  25.8 0.0 copy-done
  25.8 2.1 %gather_fusion.2 = bf16[512,1152]{1,0:T(8,128)(2,1)S(1)} fusion(bf16[768,1152]{1,0:T(8,128)(2,1)S(1)} %copy-done, s32[1024]{0:T(1024)S(1)} %pad_clamp_fusion.1), kind=kCustom, calls=%fused_computation.2 | custom fusion | bytes 2361344 | tf_op jit(solution)/shard_map/gather | solution.py:82
  27.9 1.2 reshape.77
  29.1 5.8 %all-to-all-start.2 = ((bf16[128,4,1152]{2,1,0:T(4,128)(2,1)}), bf16[128,4,1152]{2,1,0:T(4,128)(2,1)}, u32[]{:S(2)}, u32[]{:S(2)}) async-start(bf16[128,4,1152]{2,1,0:T(4,128)(2,1)} %reshape.77), calls=%async_computation.2 | async-start | bytes 2359296 | tf_op jit(solution)/shard_map/all_to_all | solution.py:85
  34.9 0.0 copy-done.1
  34.9 2.8 %gather_fusion = bf16[512,1152]{1,0:T(8,128)(2,1)} fusion(bf16[768,1152]{1,0:T(8,128)(2,1)S(1)} %copy-done.1, s32[1024]{0:T(1024)S(1)} %pad_clamp_fusion.1), kind=kCustom, calls=%fused_computation | custom fusion | bytes 2361344 | tf_op jit(solution)/shard_map/gather | solution.py:81
  37.8 3.2 %reshape.75 = bf16[128,4,1152]{2,1,0:T(4,128)(2,1)} reshape(bf16[512,1152]{1,0:T(8,128)(2,1)} %gather_fusion) | data formatting | bytes 2359296 | tf_op jit(solution)/shard_map/reshape | solution.py:81
  41.0 14.0 %all-to-all-done.2 = bf16[128,4,1152]{2,1,0:T(4,128)(2,1)} async-done(((bf16[128,4,1152]{2,1,0:T(4,128)(2,1)}), bf16[128,4,1152]{2,1,0:T(4,128)(2,1)}, u32[]{:S(2)}, u32[]{:S(2)}) %all-to-all-start.2) | async-done | bytes 1179680 | tf_op jit(solution)/shard_map/all_to_all | solution.py:85
  55.0 5.7 %all-to-all-start.1 = ((bf16[128,4,1152]{2,1,0:T(4,128)(2,1)}), bf16[128,4,1152]{2,1,0:T(4,128)(2,1)}, u32[]{:S(2)}, u32[]{:S(2)}) async-start(bf16[128,4,1152]{2,1,0:T(4,128)(2,1)} %reshape.75), calls=%async_computation.1 | async-start | bytes 2359296 | tf_op jit(solution)/shard_map/all_to_all | solution.py:84
  60.8 2.4 %reshape.78 = bf16[512,1152]{1,0:T(8,128)(2,1)S(1)} reshape(bf16[128,4,1152]{2,1,0:T(4,128)(2,1)} %all-to-all-done.2) | data formatting | bytes 2359296 | tf_op jit(solution)/shard_map/reshape | solution.py:88
  63.1 1.3 gather_fusion.3
  64.4 0.0 copy-start.2
  64.4 0.2 fusion.16
  64.6 1.0 fusion.5
  65.6 0.8 collective-permute-start
  66.4 15.2 %all-to-all-done.1 = bf16[128,4,1152]{2,1,0:T(4,128)(2,1)} async-done(((bf16[128,4,1152]{2,1,0:T(4,128)(2,1)}), bf16[128,4,1152]{2,1,0:T(4,128)(2,1)}, u32[]{:S(2)}, u32[]{:S(2)}) %all-to-all-start.1) | async-done | bytes 1179680 | tf_op jit(solution)/shard_map/all_to_all | solution.py:84
  81.7 0.0 copy-done.2
  81.7 2.4 %reshape.76 = bf16[512,1152]{1,0:T(8,128)(2,1)S(1)} reshape(bf16[128,4,1152]{2,1,0:T(4,128)(2,1)} %all-to-all-done.1) | data formatting | bytes 2359296 | tf_op jit(solution)/shard_map/reshape | solution.py:87
  84.1 1.3 gather_fusion.1
  85.3 0.2 fusion.12
  85.5 1.5 fusion.33
  87.0 5.3 %collective-permute-done = bf16[256,1152]{1,0:T(8,128)(2,1)} collective-permute-done((bf16[256,1152]{1,0:T(8,128)(2,1)}, bf16[256,1152]{1,0:T(8,128)(2,1)}, u32[]{:S(2)}, u32[]{:S(2)}) %collective-permute-start) | collective-permute-done | bytes 589856 | tf_op jit(solution)/shard_map/ppermute | solution.py:17
  92.4 0.0 collective-permute-start.1
  92.4 1.4 fusion.46
  93.8 1.5 fusion.34
  95.2 0.4 convolution_multiply_fusion.1
  95.7 6.3 %collective-permute-start.2 = (f32[256,1152]{1,0:T(8,128)S(1)}, f32[256,1152]{1,0:T(8,128)S(1)}, u32[]{:S(2)}, u32[]{:S(2)}) collective-permute-start(f32[256,1152]{1,0:T(8,128)S(1)} %convolution_multiply_fusion.1), channel_id=1, source_target_pairs={{4,0},{8,4},{12,8},{16,12},{20,16},{24,20},{28,24},{32,28},{36,32}... | collective-permute-start | bytes 3538952 | tf_op jit(solution)/shard_map/ppermute | solution.py:17
  102.0 28.6 %collective-permute-done.1 = bf16[256,1152]{1,0:T(8,128)(2,1)S(1)} collective-permute-done((bf16[256,1152]{1,0:T(8,128)(2,1)}, bf16[256,1152]{1,0:T(8,128)(2,1)S(1)}, u32[]{:S(2)}, u32[]{:S(2)}) %collective-permute-start.1) | collective-permute-done | bytes 589856 | tf_op jit(solution)/shard_map/ppermute | solution.py:17
  130.6 0.4 fusion.35
  131.0 0.4 convolution_multiply_fusion
  131.4 0.7 collective-permute-start.3
  132.1 1.4 convolution_add_fusion.1
  133.5 0.5 fusion.9
  134.0 1.3 fusion.11
  135.3 0.0 collective-permute-done.2
  135.3 23.1 %collective-permute-done.3 = f32[256,1152]{1,0:T(8,128)S(1)} collective-permute-done((f32[256,1152]{1,0:T(8,128)S(1)}, f32[256,1152]{1,0:T(8,128)S(1)}, u32[]{:S(2)}, u32[]{:S(2)}) %collective-permute-start.3) | collective-permute-done | bytes 1179680 | tf_op jit(solution)/shard_map/ppermute | solution.py:17
  158.4 0.0 copy-done.3
  158.4 0.6 fusion.13
  159.0 1.3 fusion.15
  (8 shorter events, 0.0 us)
Async XLA Ops:
  0.6 25.2 %copy-start = (bf16[768,1152]{1,0:T(8,128)(2,1)S(1)}, bf16[768,1152]{1,0:T(8,128)(2,1)}, u32[]{:S(2)}) copy-start(bf16[768,1152]{1,0:T(8,128)(2,1)} %param.5) | copy-start | bytes 5308420
  29.1 5.8 %copy-start.1 = (bf16[768,1152]{1,0:T(8,128)(2,1)S(1)}, bf16[768,1152]{1,0:T(8,128)(2,1)}, u32[]{:S(2)}) copy-start(bf16[768,1152]{1,0:T(8,128)(2,1)} %param.4) | copy-start | bytes 5308420
  29.1 26.0 %all-to-all-start.2 = ((bf16[128,4,1152]{2,1,0:T(4,128)(2,1)}), bf16[128,4,1152]{2,1,0:T(4,128)(2,1)}, u32[]{:S(2)}, u32[]{:S(2)}) async-start(bf16[128,4,1152]{2,1,0:T(4,128)(2,1)} %reshape.77), calls=%async_computation.2 | async-start | bytes 2359296 | tf_op jit(solution)/shard_map/all_to_all | solution.py:85
  55.0 26.6 %all-to-all-start.1 = ((bf16[128,4,1152]{2,1,0:T(4,128)(2,1)}), bf16[128,4,1152]{2,1,0:T(4,128)(2,1)}, u32[]{:S(2)}, u32[]{:S(2)}) async-start(bf16[128,4,1152]{2,1,0:T(4,128)(2,1)} %reshape.75), calls=%async_computation.1 | async-start | bytes 2359296 | tf_op jit(solution)/shard_map/all_to_all | solution.py:84
  64.4 17.3 %copy-start.2 = (bf16[256,1152]{1,0:T(8,128)(2,1)}, bf16[256,1152]{1,0:T(8,128)(2,1)S(1)}, u32[]{:S(2)}) copy-start(bf16[256,1152]{1,0:T(8,128)(2,1)S(1)} %gather_fusion.3) | copy-start | bytes 1769476
  65.6 26.7 %collective-permute-start = (bf16[256,1152]{1,0:T(8,128)(2,1)}, bf16[256,1152]{1,0:T(8,128)(2,1)}, u32[]{:S(2)}, u32[]{:S(2)}) collective-permute-start(bf16[256,1152]{1,0:T(8,128)(2,1)} %fusion.5), channel_id=1, source_target_pairs={{124,0},{0,4},{4,8},{8,12},{12,16},{16,20},{20,24},{24,28},{28,32}... | collective-permute-start | bytes 1769480 | tf_op jit(solution)/shard_map/ppermute | solution.py:17
  92.4 38.3 %collective-permute-start.1 = (bf16[256,1152]{1,0:T(8,128)(2,1)}, bf16[256,1152]{1,0:T(8,128)(2,1)S(1)}, u32[]{:S(2)}, u32[]{:S(2)}) collective-permute-start(bf16[256,1152]{1,0:T(8,128)(2,1)} %collective-permute-done), channel_id=1, source_target_pairs={{124,0},{0,4},{4,8},{8,12},{12,16},{16,20},{20,24},{24,28},{28,32}... | collective-permute-start | bytes 1769480 | tf_op jit(solution)/shard_map/ppermute | solution.py:17
  95.7 39.6 %collective-permute-start.2 = (f32[256,1152]{1,0:T(8,128)S(1)}, f32[256,1152]{1,0:T(8,128)S(1)}, u32[]{:S(2)}, u32[]{:S(2)}) collective-permute-start(f32[256,1152]{1,0:T(8,128)S(1)} %convolution_multiply_fusion.1), channel_id=1, source_target_pairs={{4,0},{8,4},{12,8},{16,12},{20,16},{24,20},{28,24},{32,28},{36,32}... | collective-permute-start | bytes 3538952 | tf_op jit(solution)/shard_map/ppermute | solution.py:17
  131.4 27.0 %collective-permute-start.3 = (f32[256,1152]{1,0:T(8,128)S(1)}, f32[256,1152]{1,0:T(8,128)S(1)}, u32[]{:S(2)}, u32[]{:S(2)}) collective-permute-start(f32[256,1152]{1,0:T(8,128)S(1)} %convolution_multiply_fusion), channel_id=1, source_target_pairs={{8,0},{12,4},{16,8},{20,12},{24,16},{28,20},{32,24},{36,28},{40,32... | collective-permute-start | bytes 3538952 | tf_op jit(solution)/shard_map/ppermute | solution.py:17
  134.0 24.4 %copy-start.3 = (bf16[256,1152]{1,0:T(8,128)(2,1)S(1)}, bf16[256,1152]{1,0:T(8,128)(2,1)}, u32[]{:S(2)}) copy-start(bf16[256,1152]{1,0:T(8,128)(2,1)} %copy-done.2) | copy-start | bytes 1769476
where the time goes:
time: 162 us; the launch traced here: 160 us
  waiting for transfers between devices  86.4 us (53%)
  blocking collectives  20.3 us (13%)
  starting transfers between devices  19.3 us (12%)
  local copies, waits for them, and re-layouts  18.9 us (12%)
  matrix products  9.12 us (6%)
  other arithmetic  5.47 us (3%)
    ppermute x4, waiting for transfers between devices, passed_along(): return lax.ppermute(block, axis, route)  57.1 us
    all_to_all x1, blocking collectives, shards(): lax.all_to_all(requests, ('dp', 'pool'), split_axis=0, concat_axis=0, til...  20.3 us
    all_to_all x1, waiting for transfers between devices, shards(): lax.all_to_all(image_rows, ('dp', 'pool'), split_axis=0, concat_axis=0, t...  15.2 us
    all_to_all x1, waiting for transfers between devices, shards(): lax.all_to_all(text_rows, ('dp', 'pool'), split_axis=0, concat_axis=0, ti...  14 us
    ppermute x4, starting transfers between devices, passed_along(): return lax.ppermute(block, axis, route)  7.82 us
    all_to_all x1, starting transfers between devices, shards(): lax.all_to_all(text_rows, ('dp', 'pool'), split_axis=0, concat_axis=0, ti...  5.83 us
    all_to_all x1, starting transfers between devices, shards(): lax.all_to_all(image_rows, ('dp', 'pool'), split_axis=0, concat_axis=0, t...  5.7 us
    dot_general x3, matrix products, sigmoid_weights(): lax.dot_general(image_unit, text_unit, (((1,), (1,)), ((), ())), preferre...  3.35 us
  transfers between devices with their start and end apart: 6, of which 5 were waited for; matrix products, arithmetic and copies ran while one was open for 15% of the time, Pallas kernels for 0%

commit v1 on v0

v1 whole, which is shorter than its diff:
```python
import functools
import jax
import jax.numpy as jnp
from jax import lax
from jax.experimental import pallas as pl
from jax.experimental.pallas import tpu as pltpu
from jax.sharding import PartitionSpec as P

EMBED = 1152
BLOCK = 256
POOL_DEV = 768
CHIPS = 64
SLOTS = 8
PARTS = ((0, 640), (640, 512))
MESH = pl.DeviceIdType.MESH
F32 = jnp.float32
BF16 = jnp.bfloat16

logit_scale = 10.0
logit_bias = -2.0
norm_eps = 1e-06


def dot(left, right):
    return lax.dot_general(left, right, (((1,), (0,)), ((), ())), preferred_element_type=F32)


def dot_t(left, right):
    return lax.dot_general(left, right, (((1,), (1,)), ((), ())), preferred_element_type=F32)


def iota(shape, axis):
    return lax.broadcasted_iota(jnp.int32, shape, axis)


def kernel(
    pool_image, pool_text, owners, slots,
    grad_image, grad_text,
    pools, requests, asked, picks, places, wide, out_a, out_b, back_a, back_b,
    raw, text_in, image_in, acc,
    local_sem, pool_send, pool_recv, ask_send, ask_recv, row_send, row_recv,
    ring_send, ring_recv, out_sem,
):
    a = lax.axis_index("dp")
    c = lax.axis_index("pool")
    z, x, y_lo = lax.div(a, 8), lax.rem(lax.div(a, 2), 4), lax.rem(a, 2)
    y_hi, core = lax.div(c, 2), lax.rem(c, 2)
    y = y_hi * 2 + y_lo
    chip = a * 2 + y_hi

    def partner(d):
        tz = lax.rem(z + lax.div(d, 16), 4)
        tx = lax.rem(x + lax.rem(lax.div(d, 4), 4), 4)
        ty = lax.rem(y + lax.rem(d, 4), 4)
        ta = tz * 8 + tx * 2 + lax.rem(ty, 2)
        t_hi = lax.div(ty, 2)
        return ta * 2 + t_hi, (ta, t_hi * 2 + core)

    barrier = pltpu.get_barrier_semaphore()
    sibling = (a, y_hi * 2 + 1 - core)
    pl.semaphore_signal(barrier, inc=1, device_id=sibling, device_id_type=MESH)

    def greet(d, carry):
        pl.semaphore_signal(barrier, inc=1, device_id=partner(d)[1], device_id_type=MESH)
        return carry

    lax.fori_loop(1, CHIPS, greet, 0)

    mine = pl.ds(pl.multiple_of(core * POOL_DEV, POOL_DEV), POOL_DEV)
    loads = []
    for t, source in enumerate((pool_text, pool_image)):
        loads.append(pltpu.make_async_copy(source, pools.at[t, mine], local_sem.at[t]))
        loads[-1].start()

    own_col = jnp.broadcast_to(owners[...], (BLOCK, BLOCK)).astype(F32)
    own_row = own_col.T
    same = own_col == own_row
    i0, i1 = iota((BLOCK, BLOCK), 0), iota((BLOCK, BLOCK), 1)
    rank_row = jnp.sum(jnp.where(same & (i0 < i1), 1.0, 0.0), axis=0, keepdims=True)
    rank_col = jnp.sum(jnp.where(same & (i1 < i0), 1.0, 0.0), axis=1, keepdims=True)
    place_row = (own_row[0:1] * 4.0 + rank_row).astype(jnp.int32)
    place_col = (own_col[:, 0:1] * 4.0 + rank_col).astype(jnp.int32)
    wanted = (slots[...] + POOL_DEV * lax.rem(lax.div(place_row, 4), 2)).astype(F32)
    hit = iota((CHIPS * SLOTS, BLOCK), 0) == place_row
    asking = jnp.sum(jnp.where(hit, wanted, 0.0), axis=1, keepdims=True)
    requests[...] = jnp.broadcast_to(asking, (CHIPS * SLOTS, 128)).reshape(CHIPS, SLOTS, 128)

    pl.semaphore_wait(barrier, CHIPS)
    swaps = []
    for t, source in enumerate((pool_text, pool_image)):
        swaps.append(
            pltpu.make_async_remote_copy(
                src_ref=source, dst_ref=pools.at[t, mine],
                send_sem=pool_send.at[t], recv_sem=pool_recv.at[t],
                device_id=sibling, device_id_type=MESH,
            )
        )

    def ask(d, carry):
        number, device = partner(d)
        pltpu.make_async_remote_copy(
            src_ref=requests.at[number], dst_ref=asked.at[chip],
            send_sem=ask_send, recv_sem=ask_recv,
            device_id=device, device_id_type=MESH,
        ).start()
        return carry

    lax.fori_loop(1, CHIPS, ask, 0)
    for swap in swaps:
        swap.start()
    asked[chip] = requests[chip]

    landing = lax.div(place_col, 8) * 16 + lax.rem(place_col, 8)
    columns = iota((BLOCK, CHIPS * 16), 1)
    for t in range(2):
        places[t * BLOCK:(t + 1) * BLOCK] = jnp.where(columns == landing + 8 * t, 1.0, 0.0).astype(BF16)

    others = pl.ds(0, CHIPS - 1)
    pltpu.make_async_copy(asked.at[others], asked.at[others], ask_recv).wait()
    questions = asked[...].reshape(CHIPS * SLOTS, 128)
    lane = iota((CHIPS * SLOTS, 128), 1).astype(F32)
    for j in range(2 * POOL_DEV // 128):
        picks[:, j * 128:(j + 1) * 128] = jnp.where(questions == lane + 128.0 * j, 1.0, 0.0).astype(BF16)

    for t in range(2):
        loads[t].wait()
        swaps[t].wait_recv()

    outs, backs = (out_a, out_b), (back_a, back_b)
    for p, (first, width) in enumerate(PARTS):
        for t in range(2):
            wide[t, :, 0:width] = dot(picks[...], pools[t, :, first:first + width])
        found = [wide[t, :, 0:width].reshape(CHIPS, SLOTS, width) for t in range(2)]
        outs[p][...] = jnp.concatenate(found, axis=1).astype(BF16)

        def answer(d, carry, p=p):
            number, device = partner(d)
            pltpu.make_async_remote_copy(
                src_ref=outs[p].at[number], dst_ref=backs[p].at[chip],
                send_sem=row_send.at[p], recv_sem=row_recv.at[p],
                device_id=device, device_id_type=MESH,
            ).start()
            return carry

        lax.fori_loop(1, CHIPS, answer, 0)
        backs[p][chip] = outs[p][chip]

    rings = []
    for p, (first, width) in enumerate(PARTS):
        pltpu.make_async_copy(backs[p].at[others], backs[p].at[others], row_recv.at[p]).wait()
        rows = dot(places[...], backs[p][...].reshape(CHIPS * 16, width))
        raw[:, first:first + width] = rows.astype(BF16)
        span = pl.ds(first, width)
        for k in (1, 2):
            for t, (buffer, step) in enumerate(((text_in, k), (image_in, 32 - k))):
                copy = pltpu.make_async_remote_copy(
                    src_ref=raw.at[pl.ds(t * BLOCK, BLOCK), span], dst_ref=buffer.at[k - 1, :, span],
                    send_sem=ring_send.at[p, k - 1, t], recv_sem=ring_recv.at[p, k - 1, t],
                    device_id=(lax.rem(a + step, 32), c), device_id_type=MESH,
                )
                copy.start()
                rings.append((p, k, t, copy))

    eye = i0 == i1

    def inverses(gram):
        kept = jnp.where(eye, gram, 0.0)
        return (
            lax.rsqrt(jnp.sum(kept, axis=1, keepdims=True) + norm_eps),
            lax.rsqrt(jnp.sum(kept, axis=0, keepdims=True) + norm_eps),
        )

    blocks = [raw[t * BLOCK:(t + 1) * BLOCK] for t in range(2)]
    own = [inverses(dot_t(block, block)) for block in blocks]

    def term(logits, col, row, positive):
        weights = 1.0 / (1.0 + jnp.exp(-(logit_scale * (logits * col * row) + logit_bias)))
        if positive:
            weights = weights - jnp.where(eye, 1.0, 0.0)
        return (weights * (logit_scale * row)).astype(BF16)

    for side in range(2):
        other = 1 - side
        weights = term(dot_t(blocks[side], blocks[other]), own[side][0], own[other][1], True)
        acc[side] = dot(weights, blocks[other])
    for k in (1, 2):
        for t in range(2):
            side = 1 - t
            for ring in rings:
                if ring[1] == k and ring[2] == t:
                    ring[3].wait_recv()
            block = (text_in, image_in)[t][k - 1]
            row = inverses(dot_t(block, block))[1]
            weights = term(dot_t(blocks[side], block), own[side][0], row, False)
            acc[side] += dot(weights, block)
    written = []
    for side, target in enumerate((grad_text, grad_image)):
        inverse = own[side][0]
        unit = blocks[side].astype(F32) * inverse
        total = acc[side]
        acc[side] = inverse * (total - unit * jnp.sum(unit * total, axis=-1, keepdims=True))
        written.append(pltpu.make_async_copy(acc.at[side], target, out_sem.at[side]))
        written[-1].start()

    pltpu.make_async_copy(requests.at[others], requests.at[others], ask_send).wait()
    for p in range(len(PARTS)):
        pltpu.make_async_copy(outs[p].at[others], outs[p].at[others], row_send.at[p]).wait()
    for t in range(2):
        swaps[t].wait_send()
    for ring in rings:
        ring[3].wait_send()
    for copy in written:
        copy.wait()


def shards(pool_image, pool_text, owners, slot_index):
    widths = [width for _, width in PARTS]
    gradient = jax.ShapeDtypeStruct((BLOCK, EMBED), F32)
    anywhere, vmem = pl.BlockSpec(memory_space=pl.ANY), pl.BlockSpec(memory_space=pltpu.VMEM)
    return tuple(pl.pallas_call(
        kernel,
        out_shape=(gradient, gradient),
        in_specs=[anywhere, anywhere, vmem, vmem],
        out_specs=(anywhere, anywhere),
        scratch_shapes=[
            pltpu.VMEM((2, 2 * POOL_DEV, EMBED), BF16),
            pltpu.VMEM((CHIPS, SLOTS, 128), F32),
            pltpu.VMEM((CHIPS, SLOTS, 128), F32),
            pltpu.VMEM((CHIPS * SLOTS, 2 * POOL_DEV), BF16),
            pltpu.VMEM((2 * BLOCK, CHIPS * 16), BF16),
            pltpu.VMEM((2, CHIPS * SLOTS, max(widths)), F32),
            *[pltpu.VMEM((CHIPS, 16, width), BF16) for width in widths],
            *[pltpu.VMEM((CHIPS, 16, width), BF16) for width in widths],
            pltpu.VMEM((2 * BLOCK, EMBED), BF16),
            pltpu.VMEM((2, BLOCK, EMBED), BF16),
            pltpu.VMEM((2, BLOCK, EMBED), BF16),
            pltpu.VMEM((2, BLOCK, EMBED), F32),
            pltpu.SemaphoreType.DMA((2,)),
            pltpu.SemaphoreType.DMA((2,)),
            pltpu.SemaphoreType.DMA((2,)),
            pltpu.SemaphoreType.DMA,
            pltpu.SemaphoreType.DMA,
            pltpu.SemaphoreType.DMA((len(PARTS),)),
            pltpu.SemaphoreType.DMA((len(PARTS),)),
            pltpu.SemaphoreType.DMA((len(PARTS), 2, 2)),
            pltpu.SemaphoreType.DMA((len(PARTS), 2, 2)),
            pltpu.SemaphoreType.DMA((2,)),
        ],
        compiler_params=pltpu.CompilerParams(
            collective_id=0, has_side_effects=True, vmem_limit_bytes=48 * 1024 * 1024
        ),
    )(pool_image, pool_text, owners, slot_index.reshape(1, BLOCK)))


def solution(mesh):
    in_specs = (
        P(("dp", "pool"), None),
        P(("dp", "pool"), None),
        P(("dp", "pool"), None),
        P(("dp", "pool")),
    )
    out_specs = (P(("dp", "pool"), None), P(("dp", "pool"), None))
    return jax.shard_map(shards, mesh=mesh, in_specs=in_specs, out_specs=out_specs, check_vma=False)
```

time: 162 us -> 91.8 us (0.57)
  the two profiles are of different devices: /device:TPU:0 before, /device:TPU:65 now
where the time goes in v1:
time: 91.8 us; the launch traced here: 91.6 us
  Pallas kernels  84.5 us (92%)
  local copies, waits for them, and re-layouts  6.46 us (7%)
    pallas_call x1, Pallas kernels, shards(): pl.pallas_call(kernel, out_shape=(gradient, gradient), in_specs=[anywhere...  84.5 us
    unnamed x9, local copies, waits for them, and re-layouts  6.46 us

profile of v1, /device:TPU:65, one launch (start us, length us, event | category | flops | bytes accessed | tf_op | source)
XLA Modules:
  0.0 91.6 jit_solution(10555488518044177277)
XLA Ops:
  0.6 0.8 copy.6.owners
  1.4 0.0 copy-start
  1.5 1.5 %copy-done = bf16[768,1152]{1,0:T(8,128)(2,1)S(1)} copy-done((bf16[768,1152]{1,0:T(8,128)(2,1)S(1)}, bf16[768,1152]{1,0:T(8,128)(2,1)}, u32[]{:S(2)}) %copy-start) | copy-done | bytes 1769496
  2.9 0.0 copy-start.1
  2.9 1.5 %copy-done.1 = bf16[768,1152]{1,0:T(8,128)(2,1)S(1)} copy-done((bf16[768,1152]{1,0:T(8,128)(2,1)S(1)}, bf16[768,1152]{1,0:T(8,128)(2,1)}, u32[]{:S(2)}) %copy-start.1) | copy-done | bytes 1769496
  4.4 0.0 copy-start.2
  4.4 0.7 copy-done.2
  5.1 84.5 %shard_map.59 = (f32[256,1152]{1,0:T(8,128)S(1)}, f32[256,1152]{1,0:T(8,128)S(1)}) custom-call(bf16[768,1152]{1,0:T(8,128)(2,1)S(1)} %copy-done, bf16[768,1152]{1,0:T(8,128)(2,1)S(1)} %copy-done.1, s32[256,1]{1,0:T(8,128)S(1)} %copy.6.owners, s32[1,256]{1,0:T(1,128)S(1)} %bitcast.1), custom_call_target="tpu_custom_call" | custom-call | tf_op jit(solution)/shard_map/pallas_call | solution.py:220
  89.5 1.0 %copy.9 = f32[256,1152]{1,0:T(8,128)} copy(f32[256,1152]{1,0:T(8,128)S(1)} %get-tuple-element.4) | data formatting | bytes 2359296
  90.6 1.0 %copy.10 = f32[256,1152]{1,0:T(8,128)} copy(f32[256,1152]{1,0:T(8,128)S(1)} %get-tuple-element.5) | data formatting | bytes 2359296
Async XLA Ops:
  1.4 1.5 %copy-start = (bf16[768,1152]{1,0:T(8,128)(2,1)S(1)}, bf16[768,1152]{1,0:T(8,128)(2,1)}, u32[]{:S(2)}) copy-start(bf16[768,1152]{1,0:T(8,128)(2,1)} %pool_image.1) | copy-start | bytes 5308420
  2.9 1.5 %copy-start.1 = (bf16[768,1152]{1,0:T(8,128)(2,1)S(1)}, bf16[768,1152]{1,0:T(8,128)(2,1)}, u32[]{:S(2)}) copy-start(bf16[768,1152]{1,0:T(8,128)(2,1)} %pool_text.1) | copy-start | bytes 5308420
  4.4 0.7 copy-start.2

commit v2 on v1

v2 whole, which is shorter than its diff:
```python
import jax
import jax.numpy as jnp
from jax import lax
from jax.experimental import pallas as pl
from jax.experimental.pallas import tpu as pltpu
from jax.sharding import PartitionSpec as P

EMBED = 1152
BLOCK = 256
POOL_DEV = 768
CHIPS = 64
SLOTS = 8
PARTS = ((0, 384), (384, 384), (768, 384))
ROWS = 64
LIMIT_1 = 50
LIMIT_2 = 12
MESH = pl.DeviceIdType.MESH
F32 = jnp.float32
BF16 = jnp.bfloat16

logit_scale = 10.0
logit_bias = -2.0
norm_eps = 1e-06
OFFSETS = [(dz, dx, dy) for dx in range(4) for dy in range(4) for dz in range(4)][1:]


def dot(left, right):
    return lax.dot_general(left, right, (((1,), (0,)), ((), ())), preferred_element_type=F32)


def dot_t(left, right):
    return lax.dot_general(left, right, (((1,), (1,)), ((), ())), preferred_element_type=F32)


def iota(shape, axis):
    return lax.broadcasted_iota(jnp.int32, shape, axis)


def kernel(
    pool_image, pool_text, owners, slots,
    acc, raw,
    pools, requests, heard_1, heard_2, picks, places, wide, outs, backs,
    text_in, image_in,
    local_sem, pool_send, pool_recv, ask_send, ask_recv, row_send, row_recv,
    ring_send, ring_recv,
):
    a = lax.axis_index("dp")
    c = lax.axis_index("pool")
    z, x, y_lo = lax.div(a, 8), lax.rem(lax.div(a, 2), 4), lax.rem(a, 2)
    y_hi, core = lax.div(c, 2), lax.rem(c, 2)
    y = y_hi * 2 + y_lo
    to_z = [lax.rem(z + d, 4) for d in range(4)]
    to_x = [lax.rem(x + d, 4) for d in range(4)]
    to_y = [lax.rem(y + d, 4) for d in range(4)]
    to_lo = [lax.rem(t, 2) for t in to_y]
    to_hi = [lax.div(t, 2) for t in to_y]

    def first_half(dz, dy):
        return to_z[dz] * 2 + to_lo[dy]

    def second_half(dx, dy):
        return to_x[dx] * 2 + to_hi[dy]

    def device(dz, dx, dy):
        return to_z[dz] * 8 + to_x[dx] * 2 + to_lo[dy], to_hi[dy] * 2 + core

    def number(dz, dx, dy):
        return second_half(dx, dy) * 8 + first_half(dz, dy)

    chip = number(0, 0, 0)
    sibling = (a, y_hi * 2 + 1 - core)
    group_1 = [(to_z[d] * 2 + lo, (to_z[d] * 8 + x * 2 + lo, c)) for d in range(4) for lo in (y_lo, 1 - y_lo)][1:]
    group_2 = [(to_x[d] * 2 + hi, (z * 8 + to_x[d] * 2 + y_lo, hi * 2 + core)) for d in range(4) for hi in (y_hi, 1 - y_hi)][1:]
    me_1, me_2 = z * 2 + y_lo, x * 2 + y_hi

    barrier = pltpu.get_barrier_semaphore()
    greeted = [sibling] + [member[1] for member in group_1 + group_2]
    for peer in greeted:
        pl.semaphore_signal(barrier, inc=1, device_id=peer, device_id_type=MESH)

    mine = pl.ds(pl.multiple_of(core * POOL_DEV, POOL_DEV), POOL_DEV)
    loads = []
    for t, source in enumerate((pool_text, pool_image)):
        loads.append(pltpu.make_async_copy(source, pools.at[t, mine], local_sem.at[t]))
        loads[-1].start()

    i0, i1 = iota((BLOCK, BLOCK), 0), iota((BLOCK, BLOCK), 1)
    eye = i0 == i1
    own_row = jnp.broadcast_to(owners[...], (BLOCK, BLOCK)).astype(F32)
    slot_row = jnp.broadcast_to(slots[...], (BLOCK, BLOCK)).astype(F32)
    own_col = jnp.sum(jnp.where(eye, own_row, 0.0), axis=1, keepdims=True)
    slot_col = jnp.sum(jnp.where(eye, slot_row, 0.0), axis=1, keepdims=True)
    earlier = (own_col == own_row) & (i1 < i0)
    rank = jnp.sum(jnp.where(earlier, 1.0, 0.0), axis=1, keepdims=True).astype(jnp.int32)
    owner = own_col.astype(jnp.int32)
    o_1 = (owner >> 5) * 2 + ((owner >> 2) & 1)
    o_2 = ((owner >> 3) & 3) * 2 + ((owner >> 1) & 1)
    slot = (owner & 1) * 4 + rank
    wanted = slot_col + (POOL_DEV * (owner & 1)).astype(F32)
    lanes = iota((BLOCK, 128), 1)
    place = o_1 * 128 + o_2 * SLOTS + slot
    for t in range(8):
        requests[t] = jnp.sum(jnp.where(place == lanes + 128 * t, wanted, 0.0), axis=0, keepdims=True)

    pl.semaphore_wait(barrier, len(greeted))
    swaps = []
    for t, source in enumerate((pool_text, pool_image)):
        swaps.append(
            pltpu.make_async_remote_copy(
                src_ref=source, dst_ref=pools.at[t, mine],
                send_sem=pool_send.at[t], recv_sem=pool_recv.at[t],
                device_id=sibling, device_id_type=MESH,
            )
        )

    def tell(stage, group, source, target):
        copies = []
        for i, (to, peer) in enumerate(group):
            copies.append(pltpu.make_async_remote_copy(
                src_ref=source.at[to] if stage == 0 else source, dst_ref=target,
                send_sem=ask_send.at[stage, i], recv_sem=ask_recv.at[stage, i],
                device_id=peer, device_id_type=MESH,
            ))
            copies[-1].start()
        return copies

    asks = tell(0, group_1, requests, heard_1.at[me_1])
    for swap in swaps:
        swap.start()
    heard_1[me_1] = requests[me_1]

    landing = (o_2 * 8 + o_1) * 16 + slot
    columns = iota((BLOCK, CHIPS * 16), 1)
    for t in range(2):
        places[t * BLOCK:(t + 1) * BLOCK] = jnp.where(columns == landing + 8 * t, 1.0, 0.0).astype(BF16)

    for copy in asks:
        copy.wait_recv()
    later = tell(1, group_2, heard_1, heard_2.at[me_2])
    heard_2[me_2] = heard_1[...]
    for copy in later:
        copy.wait_recv()
    asks = asks + later
    others = pl.ds(0, CHIPS - 1)
    heard = jnp.broadcast_to(heard_2[...].reshape(CHIPS, 1, 128), (CHIPS, SLOTS, 128))
    here = iota((CHIPS, SLOTS, 128), 2) - iota((CHIPS, SLOTS, 128), 1) == me_2 * SLOTS
    questions = jnp.sum(jnp.where(here, heard, 0.0), axis=2, keepdims=True).reshape(CHIPS * SLOTS, 1)
    lane = iota((CHIPS * SLOTS, 128), 1).astype(F32)
    for j in range(2 * POOL_DEV // 128):
        picks[:, j * 128:(j + 1) * 128] = jnp.where(questions == lane + 128.0 * j, 1.0, 0.0).astype(BF16)

    for t in range(2):
        loads[t].wait()
        swaps[t].wait_recv()

    for p, (first, width) in enumerate(PARTS):
        for t in range(2):
            wide[t, :, 0:width] = dot(picks[...], pools[t, :, first:first + width])
        found = [wide[t, :, 0:width].reshape(CHIPS, SLOTS, width) for t in range(2)]
        outs[p][...] = jnp.concatenate(found, axis=1).astype(BF16)
        for offset in OFFSETS:
            pltpu.make_async_remote_copy(
                src_ref=outs[p].at[number(*offset)], dst_ref=backs[p].at[chip],
                send_sem=row_send.at[p], recv_sem=row_recv.at[p],
                device_id=device(*offset), device_id_type=MESH,
            ).start()
        backs[p][chip] = outs[p][chip]

    rings = {}
    for p, (first, width) in enumerate(PARTS):
        pltpu.make_async_copy(backs[p].at[others], backs[p].at[others], row_recv.at[p]).wait()
        rows = dot(places[...], backs[p][...].reshape(CHIPS * 16, width))
        raw[:, first:first + width] = rows.astype(BF16)
        span = pl.ds(first, width)
        for k in (2, 1):
            for t, (buffer, step) in enumerate(((text_in, k), (image_in, 32 - k))):
                copy = pltpu.make_async_remote_copy(
                    src_ref=raw.at[pl.ds(t * BLOCK, BLOCK), span], dst_ref=buffer.at[k - 1, :, span],
                    send_sem=ring_send.at[p, k - 1, t], recv_sem=ring_recv.at[p, k - 1, t],
                    device_id=(lax.rem(a + step, 32), c), device_id_type=MESH,
                )
                copy.start()
                rings[p, k, t] = copy

    def finish():
        for copy in asks:
            copy.wait_send()
        for p in range(len(PARTS)):
            pltpu.make_async_copy(outs[p].at[others], outs[p].at[others], row_send.at[p]).wait()
        for t in range(2):
            swaps[t].wait_send()
        for copy in rings.values():
            copy.wait_send()

    def inverses(gram):
        kept = jnp.where(eye, gram, 0.0)
        return (
            lax.rsqrt(jnp.sum(kept, axis=1, keepdims=True) + norm_eps),
            lax.rsqrt(jnp.sum(kept, axis=0, keepdims=True) + norm_eps),
        )

    blocks = [raw[t * BLOCK:(t + 1) * BLOCK] for t in range(2)]
    own = [inverses(dot_t(block, block)) for block in blocks]

    def term(logits, col, row, positive):
        weights = 1.0 / (1.0 + jnp.exp(-(logit_scale * (logits * col * row) + logit_bias)))
        if positive:
            weights = weights - jnp.where(eye, 1.0, 0.0)
        return (weights * (logit_scale * row)).astype(BF16)

    for side in range(2):
        other = 1 - side
        weights = term(dot_t(blocks[side], blocks[other]), own[side][0], own[other][1], True)
        acc[side] = dot(weights, blocks[other])
    for k, t in ((2, 0), (2, 1), (1, 0), (1, 1)):
        side = 1 - t
        for p in range(len(PARTS)):
            rings[p, k, t].wait_recv()
        block = (text_in, image_in)[t][k - 1]
        row = inverses(dot_t(block, block))[1]
        weights = term(dot_t(blocks[side], block), own[side][0], row, False)
        acc[side] += dot(weights, block)
    finish()


def unnormalize(total, raw, grad_text, grad_image, done, sem):
    copies = []
    for t, target in enumerate((grad_text, grad_image)):
        for i in range(0, BLOCK, ROWS):
            span = pl.ds(i, ROWS)
            rows = raw[pl.ds(t * BLOCK + i, ROWS)].astype(F32)
            inverse = lax.rsqrt(jnp.sum(rows * rows, axis=-1, keepdims=True) + norm_eps)
            unit = rows * inverse
            upstream = total[t, span]
            along = jnp.sum(unit * upstream, axis=-1, keepdims=True)
            done[t, span] = inverse * (upstream - unit * along)
            copies.append(pltpu.make_async_copy(done.at[t, span], target.at[span], sem.at[t, i // ROWS]))
            copies[-1].start()
    for copy in copies:
        copy.wait()


def shards(pool_image, pool_text, owners, slot_index):
    widths = [width for _, width in PARTS]
    hbm, vmem = pl.BlockSpec(memory_space=pltpu.HBM), pl.BlockSpec(memory_space=pltpu.VMEM)
    total, raw = pl.pallas_call(
        kernel,
        out_shape=(pltpu.VMEM((2, BLOCK, EMBED), F32), pltpu.VMEM((2 * BLOCK, EMBED), BF16)),
        in_specs=[hbm, hbm, vmem, vmem],
        out_specs=(vmem, vmem),
        scratch_shapes=[
            pltpu.VMEM((2, 2 * POOL_DEV, EMBED), BF16),
            pltpu.VMEM((8, 1, 128), F32),
            pltpu.VMEM((8, 1, 128), F32),
            pltpu.VMEM((8, 8, 1, 128), F32),
            pltpu.VMEM((CHIPS * SLOTS, 2 * POOL_DEV), BF16),
            pltpu.VMEM((2 * BLOCK, CHIPS * 16), BF16),
            pltpu.VMEM((2, CHIPS * SLOTS, max(widths)), F32),
            [pltpu.VMEM((CHIPS, 16, width), BF16) for width in widths],
            [pltpu.VMEM((CHIPS, 16, width), BF16) for width in widths],
            pltpu.VMEM((2, BLOCK, EMBED), BF16),
            pltpu.VMEM((2, BLOCK, EMBED), BF16),
            pltpu.SemaphoreType.DMA((2,)),
            pltpu.SemaphoreType.DMA((2,)),
            pltpu.SemaphoreType.DMA((2,)),
            pltpu.SemaphoreType.DMA((2, 7)),
            pltpu.SemaphoreType.DMA((2, 7)),
            pltpu.SemaphoreType.DMA((len(PARTS),)),
            pltpu.SemaphoreType.DMA((len(PARTS),)),
            pltpu.SemaphoreType.DMA((len(PARTS), 2, 2)),
            pltpu.SemaphoreType.DMA((len(PARTS), 2, 2)),
        ],
        compiler_params=pltpu.CompilerParams(
            collective_id=0, has_side_effects=True, vmem_limit_bytes=LIMIT_1 * 1024 * 1024
        ),
    )(*[
        pltpu.with_memory_space_constraint(operand, pltpu.HBM)
        for operand in (pool_image, pool_text, owners.reshape(1, BLOCK), slot_index.reshape(1, BLOCK))
    ])
    grad_text, grad_image = pl.pallas_call(
        unnormalize,
        out_shape=[jax.ShapeDtypeStruct((BLOCK, EMBED), F32)] * 2,
        in_specs=[vmem, vmem],
        out_specs=[pl.BlockSpec(memory_space=pltpu.HBM)] * 2,
        scratch_shapes=[
            pltpu.VMEM((2, BLOCK, EMBED), F32),
            pltpu.SemaphoreType.DMA((2, BLOCK // ROWS)),
        ],
        compiler_params=pltpu.CompilerParams(vmem_limit_bytes=LIMIT_2 * 1024 * 1024),
    )(total, raw)
    return grad_image, grad_text


def solution(mesh):
    in_specs = (
        P(("dp", "pool"), None),
        P(("dp", "pool"), None),
        P(("dp", "pool"), None),
        P(("dp", "pool")),
    )
    out_specs = (P(("dp", "pool"), None), P(("dp", "pool"), None))
    return jax.shard_map(shards, mesh=mesh, in_specs=in_specs, out_specs=out_specs, check_vma=False)
```

time: 91.8 us -> 77.2 us (0.84)
  the two profiles are of different devices: /device:TPU:65 before, /device:TPU:0 now
where the time goes in v2:
time: 77.2 us; the launch traced here: 77.1 us
  Pallas kernels  76.5 us (99%)
    pallas_call x1, Pallas kernels, shards(): pl.pallas_call(kernel, out_shape=(pltpu.VMEM((2, BLOCK, EMBED), F32), plt...  74.5 us
    pallas_call x1, Pallas kernels, shards(): pl.pallas_call(unnormalize, out_shape=[jax.ShapeDtypeStruct((BLOCK, EMBED...  1.99 us

profile of v2, /device:TPU:0, one launch (start us, length us, event | category | flops | bytes accessed | tf_op | source)
XLA Modules:
  0.0 77.1 jit_solution(15790477983919884514)
XLA Ops:
  0.6 74.5 %shard_map.59 = (f32[2,256,1152]{2,1,0:T(8,128)S(1)}, bf16[512,1152]{1,0:T(8,128)(2,1)S(1)}) custom-call(bf16[768,1152]{1,0:T(8,128)(2,1)} %pool_image.1, bf16[768,1152]{1,0:T(8,128)(2,1)} %pool_text.1, s32[1,256]{1,0:T(1,128)} %bitcast.2, s32[1,256]{1,0:T(1,128)} %bitcast.3), custom_call_target="tpu_custom_call" | custom-call | tf_op jit(solution)/shard_map/pallas_call | solution.py:246
  75.1 2.0 %shard_map.60 = (f32[256,1152]{1,0:T(8,128)}, f32[256,1152]{1,0:T(8,128)}) custom-call(f32[2,256,1152]{2,1,0:T(8,128)S(1)} %get-tuple-element.6.total, bf16[512,1152]{1,0:T(8,128)(2,1)S(1)} %get-tuple-element.7.raw), custom_call_target="tpu_custom_call" | custom-call | tf_op jit(solution)/shard_map/pallas_call | solution.py:280

commit v3 on v2

v3 whole, which is shorter than its diff:
```python
import jax
import jax.numpy as jnp
from jax import lax
from jax.experimental import pallas as pl
from jax.experimental.pallas import tpu as pltpu
from jax.sharding import PartitionSpec as P

EMBED = 1152
BLOCK = 256
POOL_DEV = 768
CHIPS = 64
SLOTS = 8
PARTS = ((0, 256), (256, 384), (640, 512))
LAG = 2
ROWS = 64
LIMIT_1 = 50
LIMIT_2 = 12
MESH = pl.DeviceIdType.MESH
F32 = jnp.float32
BF16 = jnp.bfloat16

logit_scale = 10.0
logit_bias = -2.0
norm_eps = 1e-06
NEAR = [(dz, 0, fw, 0) for dz in range(4) for fw in range(2)][1:]
AWAY = [(0, dx, 0, fh) for dx in range(4) for fh in range(2)][1:]
FAR = [(dz, dx, fw, fh) for dx in range(4) for fh in range(2) for dz in range(4) for fw in range(2) if dx or fh]


def dot(left, right):
    return lax.dot_general(left, right, (((1,), (0,)), ((), ())), preferred_element_type=F32)


def dot_t(left, right):
    return lax.dot_general(left, right, (((1,), (1,)), ((), ())), preferred_element_type=F32)


def iota(shape, axis):
    return lax.broadcasted_iota(jnp.int32, shape, axis)


def kernel(
    pool_image, pool_text, owners, slots,
    acc, raw,
    pools, requests, heard_1, heard_2, early_picks, picks, places, early, outs, backs,
    others_in, units,
    local_sem, pool_send, pool_recv, ask_send, ask_recv, early_send, row_send, row_recv,
    ring_send, ring_recv,
):
    a = lax.axis_index("dp")
    c = lax.axis_index("pool")
    z, x, y_lo = lax.div(a, 8), lax.rem(lax.div(a, 2), 4), lax.rem(a, 2)
    y_hi, core = lax.div(c, 2), lax.rem(c, 2)
    w = lax.rem(y_lo + y_hi, 2)
    to_z = [lax.rem(z + d, 4) for d in range(4)]
    to_x = [lax.rem(x + d, 4) for d in range(4)]
    to_w, to_hi = (w, 1 - w), (y_hi, 1 - y_hi)
    to_lo = [[lax.rem(v + hi, 2) for hi in to_hi] for v in to_w]

    def first_half(way):
        return to_z[way[0]] * 2 + to_w[way[2]]

    def second_half(way):
        return to_x[way[1]] * 2 + to_hi[way[3]]

    def device(way):
        dz, dx, fw, fh = way
        return to_z[dz] * 8 + to_x[dx] * 2 + to_lo[fw][fh], to_hi[fh] * 2 + core

    def number(way):
        return second_half(way) * 8 + first_half(way)

    home = (0, 0, 0, 0)
    chip, me_1, me_2 = number(home), first_half(home), second_half(home)
    sibling = (a, y_hi * 2 + 1 - core)
    group_1 = [(first_half(way), device(way)) for way in NEAR]
    group_2 = [(second_half(way), device(way)) for way in AWAY]

    barrier = pltpu.get_barrier_semaphore()
    greeted = [sibling] + [member[1] for member in group_1 + group_2]
    for peer in greeted:
        pl.semaphore_signal(barrier, inc=1, device_id=peer, device_id_type=MESH)

    mine = pl.ds(pl.multiple_of(core * POOL_DEV, POOL_DEV), POOL_DEV)
    loads = []
    for t, source in enumerate((pool_text, pool_image)):
        loads.append(pltpu.make_async_copy(source, pools.at[t, mine], local_sem.at[t]))
        loads[-1].start()

    i0, i1 = iota((BLOCK, BLOCK), 0), iota((BLOCK, BLOCK), 1)
    eye = i0 == i1
    own_row = jnp.broadcast_to(owners[...], (BLOCK, BLOCK)).astype(F32)
    slot_row = jnp.broadcast_to(slots[...], (BLOCK, BLOCK)).astype(F32)
    own_col = jnp.sum(jnp.where(eye, own_row, 0.0), axis=1, keepdims=True)
    slot_col = jnp.sum(jnp.where(eye, slot_row, 0.0), axis=1, keepdims=True)
    earlier = (own_col == own_row) & (i1 < i0)
    rank = jnp.sum(jnp.where(earlier, 1.0, 0.0), axis=1, keepdims=True).astype(jnp.int32)
    owner = own_col.astype(jnp.int32)
    o_1 = (owner >> 5) * 2 + (((owner >> 2) + (owner >> 1)) & 1)
    o_2 = ((owner >> 3) & 3) * 2 + ((owner >> 1) & 1)
    slot = (owner & 1) * 4 + rank
    wanted = slot_col + (POOL_DEV * (owner & 1)).astype(F32)
    lanes = iota((BLOCK, 128), 1)
    place = o_1 * 128 + o_2 * SLOTS + slot
    for t in range(8):
        requests[t] = jnp.sum(jnp.where(place == lanes + 128 * t, wanted, 0.0), axis=0, keepdims=True)

    pl.semaphore_wait(barrier, len(greeted))
    swaps = []
    for p, (first, width) in enumerate(PARTS):
        span = pl.ds(first, width)
        for t, source in enumerate((pool_text, pool_image)):
            swaps.append(
                pltpu.make_async_remote_copy(
                    src_ref=source.at[:, span], dst_ref=pools.at[t, mine, span],
                    send_sem=pool_send.at[t, p], recv_sem=pool_recv.at[t, p],
                    device_id=sibling, device_id_type=MESH,
                )
            )

    def tell(stage, group, source, target):
        copies = []
        for i, (to, peer) in enumerate(group):
            copies.append(pltpu.make_async_remote_copy(
                src_ref=source.at[to] if stage == 0 else source, dst_ref=target,
                send_sem=ask_send.at[stage, i], recv_sem=ask_recv.at[stage, i],
                device_id=peer, device_id_type=MESH,
            ))
            copies[-1].start()
        return copies

    asks = tell(0, group_1, requests, heard_1.at[me_1])
    for swap in swaps:
        swap.start()
    heard_1[me_1] = requests[me_1]

    landing = (o_2 * 8 + o_1) * 16 + slot
    columns = iota((BLOCK, CHIPS * 16), 1)
    for t in range(2):
        places[t * BLOCK:(t + 1) * BLOCK] = jnp.where(columns == landing + 8 * t, 1.0, 0.0).astype(BF16)

    for copy in asks:
        copy.wait_recv()
    later = tell(1, group_2, heard_1, heard_2.at[me_2])
    heard_2[me_2] = heard_1[...]
    lane = iota((CHIPS * SLOTS, 128), 1).astype(F32)

    def pick(heard, chips, target):
        heard = jnp.broadcast_to(heard.reshape(chips, 1, 128), (chips, SLOTS, 128))
        here = iota(heard.shape, 2) - iota(heard.shape, 1) == me_2 * SLOTS
        questions = jnp.sum(jnp.where(here, heard, 0.0), axis=2, keepdims=True).reshape(chips * SLOTS, 1)
        for j in range(2 * POOL_DEV // 128):
            hits = questions == lane[:chips * SLOTS] + 128.0 * j
            target[:, j * 128:(j + 1) * 128] = jnp.where(hits, 1.0, 0.0).astype(BF16)

    def found(picked, chips, first, width):
        rows = [dot(picked[...], pools[t, :, first:first + width]) for t in range(2)]
        return jnp.concatenate([r.reshape(chips, SLOTS, width) for r in rows], axis=1).astype(BF16)

    def answer(source, p, way, sem):
        return pltpu.make_async_remote_copy(
            src_ref=source, dst_ref=backs[p].at[chip], send_sem=sem, recv_sem=row_recv.at[p],
            device_id=device(way), device_id_type=MESH,
        )

    pick(heard_1[...], 8, early_picks)
    for copy in loads:
        copy.wait()
    for p, (first, width) in enumerate(PARTS):
        for swap in swaps[2 * p:2 * p + 2]:
            swap.wait_recv()
        early[p][...] = found(early_picks, 8, first, width)
        for way in NEAR:
            answer(early[p].at[first_half(way)], p, way, early_send.at[p]).start()
        backs[p][chip] = early[p][me_1]

    for copy in later:
        copy.wait_recv()
    asks = asks + later
    others = pl.ds(0, CHIPS - 1)
    far = pl.ds(0, len(FAR))
    near = pl.ds(0, len(NEAR))
    pick(heard_2[...], CHIPS, picks)
    for p, (first, width) in enumerate(PARTS):
        outs[p][...] = found(picks, CHIPS, first, width)
        for way in FAR:
            answer(outs[p].at[number(way)], p, way, row_send.at[p]).start()

    odd = lax.rem(a, 2)
    neighbour = (a + 1 - 2 * odd, c)
    rings = {}

    def ring(p, role, source, target, peer):
        span = pl.ds(PARTS[p][0], PARTS[p][1])
        rings[p, role] = pltpu.make_async_remote_copy(
            src_ref=source.at[:, span], dst_ref=target.at[:, span],
            send_sem=ring_send.at[p, role], recv_sem=ring_recv.at[p, role],
            device_id=peer, device_id_type=MESH,
        )
        rings[p, role].start()

    def own_block(t):
        return raw.at[pl.ds(pl.multiple_of(t * BLOCK, BLOCK), BLOCK)]

    def pass_on(p):
        rings[p, 0].wait_recv()
        ring(p, 3, others_in.at[1 - odd, 1], others_in.at[1 - odd, 0], neighbour)

    for p, (first, width) in enumerate(PARTS):
        pltpu.make_async_copy(backs[p].at[others], backs[p].at[others], row_recv.at[p]).wait()
        rows = dot(places[...], backs[p][...].reshape(CHIPS * 16, width))
        raw[:, first:first + width] = rows.astype(BF16)
        for role, t in ((0, 1 - odd), (1, odd)):
            ring(p, role, own_block(t), others_in.at[t, 1], (lax.rem(a + 2 + 28 * t, 32), c))
        ring(p, 2, own_block(odd), others_in.at[odd, 0], neighbour)
        if p >= LAG:
            pass_on(p - LAG)
    for p in range(len(PARTS) - LAG, len(PARTS)):
        pass_on(p)

    def finish():
        for copy in asks:
            copy.wait_send()
        for p in range(len(PARTS)):
            pltpu.make_async_copy(outs[p].at[far], outs[p].at[far], row_send.at[p]).wait()
            pltpu.make_async_copy(early[p].at[near], early[p].at[near], early_send.at[p]).wait()
        for swap in swaps:
            swap.wait_send()
        for copy in rings.values():
            copy.wait_send()

    def normalized(block):
        rows = block.astype(F32)
        return (rows * lax.rsqrt(jnp.sum(rows * rows, axis=-1, keepdims=True) + norm_eps)).astype(BF16)

    def weights(left, right, positive):
        values = 1.0 / (1.0 + jnp.exp(-(logit_scale * dot_t(left, right) + logit_bias)))
        if positive:
            values = values - jnp.where(eye, 1.0, 0.0)
        return values.astype(BF16)

    for t in range(2):
        units[t] = normalized(raw[t * BLOCK:(t + 1) * BLOCK])
    for side in range(2):
        acc[side] = dot(weights(units[side], units[1 - side], True), units[1 - side])
    for role, t, k in ((0, 1 - odd, 2), (1, odd, 2), (2, 1 - odd, 1), (3, odd, 1)):
        if role:
            for p in range(len(PARTS)):
                rings[p, role].wait_recv()
        block = normalized(others_in[t, k - 1])
        acc[1 - t] += dot(weights(units[1 - t], block, False), block)
    finish()


def unnormalize(total, raw, grad_text, grad_image, done, sem):
    copies = []
    for t, target in enumerate((grad_text, grad_image)):
        for i in range(0, BLOCK, ROWS):
            span = pl.ds(i, ROWS)
            rows = raw[pl.ds(t * BLOCK + i, ROWS)].astype(F32)
            inverse = lax.rsqrt(jnp.sum(rows * rows, axis=-1, keepdims=True) + norm_eps)
            unit = rows * inverse
            upstream = logit_scale * total[t, span]
            along = jnp.sum(unit * upstream, axis=-1, keepdims=True)
            done[t, span] = inverse * (upstream - unit * along)
            copies.append(pltpu.make_async_copy(done.at[t, span], target.at[span], sem.at[t, i // ROWS]))
            copies[-1].start()
    for copy in copies:
        copy.wait()


def shards(pool_image, pool_text, owners, slot_index):
    widths = [width for _, width in PARTS]
    hbm, vmem = pl.BlockSpec(memory_space=pltpu.HBM), pl.BlockSpec(memory_space=pltpu.VMEM)
    total, raw = pl.pallas_call(
        kernel,
        out_shape=(pltpu.VMEM((2, BLOCK, EMBED), F32), pltpu.VMEM((2 * BLOCK, EMBED), BF16)),
        in_specs=[hbm, hbm, vmem, vmem],
        out_specs=(vmem, vmem),
        scratch_shapes=[
            pltpu.VMEM((2, 2 * POOL_DEV, EMBED), BF16),
            pltpu.VMEM((8, 1, 128), F32),
            pltpu.VMEM((8, 1, 128), F32),
            pltpu.VMEM((8, 8, 1, 128), F32),
            pltpu.VMEM((8 * SLOTS, 2 * POOL_DEV), BF16),
            pltpu.VMEM((CHIPS * SLOTS, 2 * POOL_DEV), BF16),
            pltpu.VMEM((2 * BLOCK, CHIPS * 16), BF16),
            [pltpu.VMEM((8, 16, width), BF16) for width in widths],
            [pltpu.VMEM((CHIPS, 16, width), BF16) for width in widths],
            [pltpu.VMEM((CHIPS, 16, width), BF16) for width in widths],
            pltpu.VMEM((2, 2, BLOCK, EMBED), BF16),
            pltpu.VMEM((2, BLOCK, EMBED), BF16),
            pltpu.SemaphoreType.DMA((2,)),
            pltpu.SemaphoreType.DMA((2, len(PARTS))),
            pltpu.SemaphoreType.DMA((2, len(PARTS))),
            pltpu.SemaphoreType.DMA((2, 7)),
            pltpu.SemaphoreType.DMA((2, 7)),
            pltpu.SemaphoreType.DMA((len(PARTS),)),
            pltpu.SemaphoreType.DMA((len(PARTS),)),
            pltpu.SemaphoreType.DMA((len(PARTS),)),
            pltpu.SemaphoreType.DMA((len(PARTS), 4)),
            pltpu.SemaphoreType.DMA((len(PARTS), 4)),
        ],
        compiler_params=pltpu.CompilerParams(
            collective_id=0, has_side_effects=True, vmem_limit_bytes=LIMIT_1 * 1024 * 1024
        ),
    )(*[
        pltpu.with_memory_space_constraint(operand, pltpu.HBM)
        for operand in (pool_image, pool_text, owners.reshape(1, BLOCK), slot_index.reshape(1, BLOCK))
    ])
    grad_text, grad_image = pl.pallas_call(
        unnormalize,
        out_shape=[jax.ShapeDtypeStruct((BLOCK, EMBED), F32)] * 2,
        in_specs=[vmem, vmem],
        out_specs=[pl.BlockSpec(memory_space=pltpu.HBM)] * 2,
        scratch_shapes=[
            pltpu.VMEM((2, BLOCK, EMBED), F32),
            pltpu.SemaphoreType.DMA((2, BLOCK // ROWS)),
        ],
        compiler_params=pltpu.CompilerParams(vmem_limit_bytes=LIMIT_2 * 1024 * 1024),
    )(total, raw)
    return grad_image, grad_text


def solution(mesh):
    in_specs = (
        P(("dp", "pool"), None),
        P(("dp", "pool"), None),
        P(("dp", "pool"), None),
        P(("dp", "pool")),
    )
    out_specs = (P(("dp", "pool"), None), P(("dp", "pool"), None))
    return jax.shard_map(shards, mesh=mesh, in_specs=in_specs, out_specs=out_specs, check_vma=False)
```

time: 77.2 us -> 70.4 us (0.912)
  Pallas kernels: 76.5 us -> 69.6 us
    pallas_call x1, Pallas kernels: 74.5 us -> 67.5 us  [shards(): pl.pallas_call(kernel, out_shape=(pltpu.VMEM((2, BLOCK, EMBED), F32), plt...]
where the time goes in v3:
time: 70.4 us; the launch traced here: 70.3 us
  Pallas kernels  69.6 us (99%)
    pallas_call x1, Pallas kernels, shards(): pl.pallas_call(kernel, out_shape=(pltpu.VMEM((2, BLOCK, EMBED), F32), plt...  67.5 us
    pallas_call x1, Pallas kernels, shards(): pl.pallas_call(unnormalize, out_shape=[jax.ShapeDtypeStruct((BLOCK, EMBED...  2.07 us

profile of v3, /device:TPU:0, one launch (start us, length us, event | category | flops | bytes accessed | tf_op | source)
XLA Modules:
  0.0 70.3 jit_solution(2185087280744350449)
XLA Ops:
  0.6 67.5 %shard_map.59 = (f32[2,256,1152]{2,1,0:T(8,128)S(1)}, bf16[512,1152]{1,0:T(8,128)(2,1)S(1)}) custom-call(bf16[768,1152]{1,0:T(8,128)(2,1)} %pool_image.1, bf16[768,1152]{1,0:T(8,128)(2,1)} %pool_text.1, s32[1,256]{1,0:T(1,128)} %bitcast.2, s32[1,256]{1,0:T(1,128)} %bitcast.3), custom_call_target="tpu_custom_call" | custom-call | tf_op jit(solution)/shard_map/pallas_call | solution.py:275
  68.2 2.1 %shard_map.60 = (f32[256,1152]{1,0:T(8,128)}, f32[256,1152]{1,0:T(8,128)}) custom-call(f32[2,256,1152]{2,1,0:T(8,128)S(1)} %get-tuple-element.6.total, bf16[512,1152]{1,0:T(8,128)(2,1)S(1)} %get-tuple-element.7.raw), custom_call_target="tpu_custom_call" | custom-call | tf_op jit(solution)/shard_map/pallas_call | solution.py:311

commit v4 on v3

--- a/solution.py
+++ b/solution.py
@@ -10,7 +10,7 @@
 POOL_DEV = 768
 CHIPS = 64
 SLOTS = 8
-PARTS = ((0, 256), (256, 384), (640, 512))
+PARTS = ((0, 256), (256, 512), (768, 384))
 LAG = 2
 ROWS = 64
 LIMIT_1 = 50
@@ -39,12 +39,20 @@
     return lax.broadcasted_iota(jnp.int32, shape, axis)
 
 
+def unnormalized(block, total):
+    rows = block.astype(F32)
+    inverse = lax.rsqrt(jnp.sum(rows * rows, axis=-1, keepdims=True) + norm_eps)
+    unit = rows * inverse
+    upstream = logit_scale * total
+    return inverse * (upstream - unit * jnp.sum(unit * upstream, axis=-1, keepdims=True))
+
+
 def kernel(
-    pool_image, pool_text, owners, slots,
+    pool_image, pool_text, owners_at, slots_at,
     acc, raw,
-    pools, requests, heard_1, heard_2, early_picks, picks, places, early, outs, backs,
+    owners, slots, pools, requests, heard_1, heard_2, early_picks, picks, places, early, outs, backs,
     others_in, units,
-    local_sem, pool_send, pool_recv, ask_send, ask_recv, early_send, row_send, row_recv,
+    name_sem, local_sem, pool_send, pool_recv, ask_send, ask_recv, early_send, row_send, row_recv,
     ring_send, ring_recv,
 ):
     a = lax.axis_index("dp")
@@ -76,6 +84,10 @@
     group_1 = [(first_half(way), device(way)) for way in NEAR]
     group_2 = [(second_half(way), device(way)) for way in AWAY]
 
+    names = []
+    for i, (source, target) in enumerate(((owners_at, owners), (slots_at, slots))):
+        names.append(pltpu.make_async_copy(source, target, name_sem.at[i]))
+        names[-1].start()
     barrier = pltpu.get_barrier_semaphore()
     greeted = [sibling] + [member[1] for member in group_1 + group_2]
     for peer in greeted:
@@ -87,6 +99,8 @@
         loads.append(pltpu.make_async_copy(source, pools.at[t, mine], local_sem.at[t]))
         loads[-1].start()
 
+    for copy in names:
+        copy.wait()
     i0, i1 = iota((BLOCK, BLOCK), 0), iota((BLOCK, BLOCK), 1)
     eye = i0 == i1
     own_row = jnp.broadcast_to(owners[...], (BLOCK, BLOCK)).astype(F32)
@@ -249,24 +263,31 @@
                 rings[p, role].wait_recv()
         block = normalized(others_in[t, k - 1])
         acc[1 - t] += dot(weights(units[1 - t], block, False), block)
+        if role == 2:
+            for i in range(0, BLOCK, ROWS):
+                span = pl.ds(i, ROWS)
+                at = pl.ds(pl.multiple_of(odd * BLOCK + i, ROWS), ROWS)
+                acc[odd, span] = unnormalized(raw[at], acc[odd, span])
     finish()
 
 
-def unnormalize(total, raw, grad_text, grad_image, done, sem):
-    copies = []
-    for t, target in enumerate((grad_text, grad_image)):
-        for i in range(0, BLOCK, ROWS):
-            span = pl.ds(i, ROWS)
-            rows = raw[pl.ds(t * BLOCK + i, ROWS)].astype(F32)
-            inverse = lax.rsqrt(jnp.sum(rows * rows, axis=-1, keepdims=True) + norm_eps)
-            unit = rows * inverse
-            upstream = logit_scale * total[t, span]
-            along = jnp.sum(unit * upstream, axis=-1, keepdims=True)
-            done[t, span] = inverse * (upstream - unit * along)
-            copies.append(pltpu.make_async_copy(done.at[t, span], target.at[span], sem.at[t, i // ROWS]))
-            copies[-1].start()
-    for copy in copies:
-        copy.wait()
+def write(total, raw, grad_text, grad_image, done, sem):
+    odd = lax.rem(lax.axis_index("dp"), 2)
+    targets = (grad_text, grad_image)
+    for side in range(2):
+
+        @pl.when(odd == side)
+        def _():
+            whole = pltpu.make_async_copy(total.at[side], targets[side], sem.at[0])
+            whole.start()
+            copies = [whole]
+            for i in range(0, BLOCK, ROWS):
+                span = pl.ds(i, ROWS)
+                done[span] = unnormalized(raw[pl.ds((1 - side) * BLOCK + i, ROWS)], total[1 - side, span])
+                copies.append(pltpu.make_async_copy(done.at[span], targets[1 - side].at[span], sem.at[1 + i // ROWS]))
+                copies[-1].start()
+            for copy in copies:
+                copy.wait()
 
 
 def shards(pool_image, pool_text, owners, slot_index):
@@ -275,9 +296,11 @@
     total, raw = pl.pallas_call(
         kernel,
         out_shape=(pltpu.VMEM((2, BLOCK, EMBED), F32), pltpu.VMEM((2 * BLOCK, EMBED), BF16)),
-        in_specs=[hbm, hbm, vmem, vmem],
+        in_specs=[hbm] * 4,
         out_specs=(vmem, vmem),
         scratch_shapes=[
+            pltpu.VMEM((1, BLOCK), jnp.int32),
+            pltpu.VMEM((1, BLOCK), jnp.int32),
             pltpu.VMEM((2, 2 * POOL_DEV, EMBED), BF16),
             pltpu.VMEM((8, 1, 128), F32),
             pltpu.VMEM((8, 1, 128), F32),
@@ -290,6 +313,7 @@
             [pltpu.VMEM((CHIPS, 16, width), BF16) for width in widths],
             pltpu.VMEM((2, 2, BLOCK, EMBED), BF16),
             pltpu.VMEM((2, BLOCK, EMBED), BF16),
+            pltpu.SemaphoreType.DMA((2,)),
             pltpu.SemaphoreType.DMA((2,)),
             pltpu.SemaphoreType.DMA((2, len(PARTS))),
             pltpu.SemaphoreType.DMA((2, len(PARTS))),
@@ -309,13 +333,13 @@
         for operand in (pool_image, pool_text, owners.reshape(1, BLOCK), slot_index.reshape(1, BLOCK))
     ])
     grad_text, grad_image = pl.pallas_call(
-        unnormalize,
+        write,
         out_shape=[jax.ShapeDtypeStruct((BLOCK, EMBED), F32)] * 2,
         in_specs=[vmem, vmem],
         out_specs=[pl.BlockSpec(memory_space=pltpu.HBM)] * 2,
         scratch_shapes=[
-            pltpu.VMEM((2, BLOCK, EMBED), F32),
-            pltpu.SemaphoreType.DMA((2, BLOCK // ROWS)),
+            pltpu.VMEM((BLOCK, EMBED), F32),
+            pltpu.SemaphoreType.DMA((1 + BLOCK // ROWS,)),
         ],
         compiler_params=pltpu.CompilerParams(vmem_limit_bytes=LIMIT_2 * 1024 * 1024),
     )(total, raw)

time: 70.4 us -> 68.6 us (0.974)
  Pallas kernels: 69.6 us -> 67.8 us
    pallas_call x1, Pallas kernels: 67.5 us -> 66.4 us  [shards(): pl.pallas_call(kernel, out_shape=(pltpu.VMEM((2, BLOCK, EMBED), F32), plt...]
where the time goes in v4:
time: 68.6 us; the launch traced here: 68.5 us
  Pallas kernels  67.8 us (99%)
    pallas_call x1, Pallas kernels, shards(): pl.pallas_call(kernel, out_shape=(pltpu.VMEM((2, BLOCK, EMBED), F32), plt...  66.4 us
    pallas_call x1, Pallas kernels, shards(): pl.pallas_call(write, out_shape=[jax.ShapeDtypeStruct((BLOCK, EMBED), F32...  1.45 us

profile of v4, /device:TPU:0, one launch (start us, length us, event | category | flops | bytes accessed | tf_op | source)
XLA Modules:
  0.0 68.5 jit_solution(10205701101916483550)
XLA Ops:
  0.6 66.4 %shard_map.59 = (f32[2,256,1152]{2,1,0:T(8,128)S(1)}, bf16[512,1152]{1,0:T(8,128)(2,1)S(1)}) custom-call(bf16[768,1152]{1,0:T(8,128)(2,1)} %pool_image.1, bf16[768,1152]{1,0:T(8,128)(2,1)} %pool_text.1, s32[1,256]{1,0:T(1,128)} %bitcast.2, s32[1,256]{1,0:T(1,128)} %bitcast.3), custom_call_target="tpu_custom_call" | custom-call | tf_op jit(solution)/shard_map/pallas_call | solution.py:296
  67.0 1.5 %shard_map.60 = (f32[256,1152]{1,0:T(8,128)}, f32[256,1152]{1,0:T(8,128)}) custom-call(f32[2,256,1152]{2,1,0:T(8,128)S(1)} %get-tuple-element.6.total, bf16[512,1152]{1,0:T(8,128)(2,1)S(1)} %get-tuple-element.7.raw), custom_call_target="tpu_custom_call" | custom-call | tf_op jit(solution)/shard_map/pallas_call | solution.py:335

commit v5 on v4

--- a/solution.py
+++ b/solution.py
@@ -24,7 +24,7 @@
 norm_eps = 1e-06
 NEAR = [(dz, 0, fw, 0) for dz in range(4) for fw in range(2)][1:]
 AWAY = [(0, dx, 0, fh) for dx in range(4) for fh in range(2)][1:]
-FAR = [(dz, dx, fw, fh) for dx in range(4) for fh in range(2) for dz in range(4) for fw in range(2) if dx or fh]
+FAR = [(dz, dx, fw, fh) for dz in range(4) for fh in range(2) for dx in range(4) for fw in range(2) if dx or fh]
 
 
 def dot(left, right):

time: 68.6 us -> 68.2 us (level)
  no operation moved by 1% of the time
where the time goes in v5:
time: 68.2 us; the launch traced here: 68.1 us
  Pallas kernels  67.4 us (99%)
    pallas_call x1, Pallas kernels, shards(): pl.pallas_call(kernel, out_shape=(pltpu.VMEM((2, BLOCK, EMBED), F32), plt...  66 us
    pallas_call x1, Pallas kernels, shards(): pl.pallas_call(write, out_shape=[jax.ShapeDtypeStruct((BLOCK, EMBED), F32...  1.45 us

profile of v5, /device:TPU:0, one launch (start us, length us, event | category | flops | bytes accessed | tf_op | source)
XLA Modules:
  0.0 68.1 jit_solution(1258849633572593841)
XLA Ops:
  0.6 66.0 %shard_map.59 = (f32[2,256,1152]{2,1,0:T(8,128)S(1)}, bf16[512,1152]{1,0:T(8,128)(2,1)S(1)}) custom-call(bf16[768,1152]{1,0:T(8,128)(2,1)} %pool_image.1, bf16[768,1152]{1,0:T(8,128)(2,1)} %pool_text.1, s32[1,256]{1,0:T(1,128)} %bitcast.2, s32[1,256]{1,0:T(1,128)} %bitcast.3), custom_call_target="tpu_custom_call" | custom-call | tf_op jit(solution)/shard_map/pallas_call | solution.py:296
  66.6 1.5 %shard_map.60 = (f32[256,1152]{1,0:T(8,128)}, f32[256,1152]{1,0:T(8,128)}) custom-call(f32[2,256,1152]{2,1,0:T(8,128)S(1)} %get-tuple-element.6.total, bf16[512,1152]{1,0:T(8,128)(2,1)S(1)} %get-tuple-element.7.raw), custom_call_target="tpu_custom_call" | custom-call | tf_op jit(solution)/shard_map/pallas_call | solution.py:335

commit v6 on v5

--- a/solution.py
+++ b/solution.py
@@ -12,7 +12,7 @@
 SLOTS = 8
 PARTS = ((0, 256), (256, 512), (768, 384))
 LAG = 2
-ROWS = 64
+ROWS = 32
 LIMIT_1 = 50
 LIMIT_2 = 12
 MESH = pl.DeviceIdType.MESH
@@ -229,7 +229,7 @@
         ring(p, 2, own_block(odd), others_in.at[odd, 0], neighbour)
         if p >= LAG:
             pass_on(p - LAG)
-    for p in range(len(PARTS) - LAG, len(PARTS)):
+    for p in range(len(PARTS) - LAG, len(PARTS) - 1):
         pass_on(p)
 
     def finish():
@@ -257,6 +257,7 @@
         units[t] = normalized(raw[t * BLOCK:(t + 1) * BLOCK])
     for side in range(2):
         acc[side] = dot(weights(units[side], units[1 - side], True), units[1 - side])
+    pass_on(len(PARTS) - 1)
     for role, t, k in ((0, 1 - odd, 2), (1, odd, 2), (2, 1 - odd, 1), (3, odd, 1)):
         if role:
             for p in range(len(PARTS)):

time: 68.2 us -> 68.2 us (level)
  no operation moved by 1% of the time
where the time goes in v6:
time: 68.2 us; the launch traced here: 68.1 us
  Pallas kernels  67.5 us (99%)
    pallas_call x1, Pallas kernels, shards(): pl.pallas_call(kernel, out_shape=(pltpu.VMEM((2, BLOCK, EMBED), F32), plt...  66 us
    pallas_call x1, Pallas kernels, shards(): pl.pallas_call(write, out_shape=[jax.ShapeDtypeStruct((BLOCK, EMBED), F32...  1.48 us

profile of v6, /device:TPU:0, one launch (start us, length us, event | category | flops | bytes accessed | tf_op | source)
XLA Modules:
  0.0 68.1 jit_solution(10734924838778949741)
XLA Ops:
  0.6 66.0 %shard_map.59 = (f32[2,256,1152]{2,1,0:T(8,128)S(1)}, bf16[512,1152]{1,0:T(8,128)(2,1)S(1)}) custom-call(bf16[768,1152]{1,0:T(8,128)(2,1)} %pool_image.1, bf16[768,1152]{1,0:T(8,128)(2,1)} %pool_text.1, s32[1,256]{1,0:T(1,128)} %bitcast.2, s32[1,256]{1,0:T(1,128)} %bitcast.3), custom_call_target="tpu_custom_call" | custom-call | tf_op jit(solution)/shard_map/pallas_call | solution.py:297
  66.6 1.5 %shard_map.60 = (f32[256,1152]{1,0:T(8,128)}, f32[256,1152]{1,0:T(8,128)}) custom-call(f32[2,256,1152]{2,1,0:T(8,128)S(1)} %get-tuple-element.6.total, bf16[512,1152]{1,0:T(8,128)(2,1)S(1)} %get-tuple-element.7.raw), custom_call_target="tpu_custom_call" | custom-call | tf_op jit(solution)/shard_map/pallas_call | solution.py:336
